TPU v7x, 256 devices: a whole 4x4x8 slice. The times are simulated.
256 devices in a mesh: head: 8 (over x_hi, y), blk: 32 (over x_lo, z, core).
Axes of the slice: x: 4 (x_hi: 2, x_lo: 2; x = x_hi * 2 + x_lo), y: 4, z: 8, core: 2. Of those that a mesh axis runs over, the one named last changes fastest.
Arguments:
- queries: bfloat16 [64, 128, 2048], P('blk', None, 'head'), may hold values from -8 to 8
- key_vectors: bfloat16 [64, 128, 2048], P('blk', None, 'head'), may hold values from -8 to 8
- value_vectors: bfloat16 [64, 128, 2048], P('blk', None, 'head'), may hold values from -6 to 6
- out_grad: bfloat16 [64, 128, 2048], P('blk', None, 'head'), may hold values from -6 to 6
- block_order: int32 [64], replicated, may hold values from 0 to 63, each once
Outputs:
- attended: bfloat16 [64, 128, 2048], P('blk')
- query_grad: bfloat16 [64, 128, 2048], P('blk', None, 'head')
- key_grad: bfloat16 [64, 128, 2048], P('blk', None, 'head')
- value_grad: bfloat16 [64, 128, 2048], P('blk', None, 'head')
Inputs may be any that keep to these rules, and one draw needn't show every extreme that they name: `block_order`: a permutation of the 64 block numbers.
All inputs are finite; a program needn't handle non-finite values.
Results may differ from a plain program's by a relative error of at most 0.03.
Values may be sent and summed in bfloat16 or wider, within the bound.
A program may use at most 64 MiB of HBM per device.

v0:
```python
import jax
import jax.numpy as jnp
from jax import lax
from jax.sharding import PartitionSpec as P

DH = 128


block_rows = 512
neg_large = -1e30


def block_positions(block_order, span_rows, offset, amount):
    row_index = offset + jnp.arange(amount, dtype=jnp.int32)
    slot_index = row_index // span_rows
    matches = slot_index[:, None] == jnp.arange(block_order.shape[0], dtype=jnp.int32)[None, :]
    chosen = jnp.sum(jnp.where(matches, block_order[None, :], 0), axis=1)
    return chosen * span_rows + row_index % span_rows


def in_blocks(update, running, pieces):
    piece_rows = pieces[0].shape[0]
    blocks = piece_rows // block_rows
    stacked = tuple((array.reshape((blocks, block_rows) + array.shape[1:]) for array in pieces))
    starts = block_rows * jnp.arange(blocks, dtype=jnp.int32)

    def visiting(current, scanned):
        pieces_now, first_row = scanned
        return (update(current, pieces_now, first_row), None)

    finished, unused = lax.scan(visiting, running, (stacked, starts))
    return finished


def visible_of(query_pos, key_pos):
    return key_pos[None, :] <= query_pos[:, None]


def body(queries, key_vectors, value_vectors, out_grad, block_order):
    cycle_index = lax.axis_index("blk")
    span_rows = queries.shape[1]
    local_rows = 2 * span_rows
    local_heads = queries.shape[2] // DH
    score_scale = DH ** (-0.5)

    def flatten(array):
        return array.reshape(local_rows, local_heads, DH)

    flat_q = flatten(queries)
    flat_k = flatten(key_vectors)
    flat_v = flatten(value_vectors)
    flat_g = flatten(out_grad)
    my_positions = block_positions(block_order, span_rows, cycle_index * local_rows, local_rows)

    def scores_of(query_part, key_part, visible):
        scores = (
            jnp.einsum("qhd,khd->hqk", query_part, key_part, preferred_element_type=jnp.float32)
            * score_scale
        )
        return jnp.where(visible[None], scores, neg_large)

    def attend_block(running, pieces, offset):
        key_part, value_part = pieces
        visible = visible_of(
            my_positions, block_positions(block_order, span_rows, offset, key_part.shape[0])
        )
        row_max, row_sum, weighted = running
        scores = scores_of(flat_q, key_part, visible)
        new_max = jnp.maximum(row_max, jnp.max(scores, axis=2))
        probs = jnp.where(visible[None], jnp.exp(scores - new_max[..., None]), 0.0)
        rescale = jnp.exp(row_max - new_max)
        new_sum = row_sum * rescale + jnp.sum(probs, axis=2)
        update = jnp.einsum(
            "hqk,khd->hqd",
            probs,
            value_part.astype(jnp.float32),
            preferred_element_type=jnp.float32,
            precision=lax.Precision.HIGHEST,
        )
        return (new_max, new_sum, weighted * rescale[..., None] + update)

    zeros_heads = jnp.zeros((local_heads, local_rows, DH), jnp.float32)
    zeros_rows = jnp.zeros((local_rows, local_heads, DH), jnp.float32)
    initial = (
        jnp.full((local_heads, local_rows), neg_large, jnp.float32),
        jnp.zeros((local_heads, local_rows), jnp.float32),
        zeros_heads,
    )
    row_max, row_sum, weighted = in_blocks(
        attend_block,
        initial,
        (
            lax.all_gather(flat_k, "blk", axis=0, tiled=True),
            lax.all_gather(flat_v, "blk", axis=0, tiled=True),
        ),
    )
    log_total = row_max + jnp.log(row_sum)
    attended = (weighted / row_sum[..., None]).astype(jnp.bfloat16)
    attended_rows = jnp.transpose(attended, (1, 0, 2)).reshape(2, span_rows, local_heads * DH)
    attended_all = lax.all_gather(attended_rows, "head", axis=2, tiled=True)
    grad_heads = jnp.transpose(flat_g, (1, 0, 2)).astype(jnp.float32)
    row_delta = jnp.sum(grad_heads * attended.astype(jnp.float32), axis=2)

    def gradient_terms(query_part, grad_part, lse_part, delta_part, key_part, value_part, visible):
        scores = scores_of(query_part, key_part, visible)
        probs = jnp.where(visible[None], jnp.exp(scores - lse_part[..., None]), 0.0)
        dprob = jnp.einsum(
            "qhd,khd->hqk", grad_part, value_part, preferred_element_type=jnp.float32
        )
        dscore = (probs * (dprob - delta_part[..., None]) * score_scale).astype(jnp.bfloat16)
        return (probs.astype(jnp.bfloat16), dscore)

    def query_block(running, pieces, offset):
        key_part, value_part = pieces
        visible = visible_of(
            my_positions, block_positions(block_order, span_rows, offset, key_part.shape[0])
        )
        probs_low, dscore = gradient_terms(
            flat_q, flat_g, log_total, row_delta, key_part, value_part, visible
        )
        return running + jnp.einsum(
            "hqk,khd->hqd", dscore, key_part, preferred_element_type=jnp.float32
        )

    def key_block_with(lse_all, delta_all):

        def key_block(running, pieces, offset):
            query_part, grad_part = pieces
            amount = query_part.shape[0]
            visible = visible_of(
                block_positions(block_order, span_rows, offset, amount), my_positions
            )
            lse_part = lax.dynamic_slice_in_dim(lse_all, offset, amount, 0).T
            delta_part = lax.dynamic_slice_in_dim(delta_all, offset, amount, 0).T
            key_total, value_total = running
            probs_low, dscore = gradient_terms(
                query_part, grad_part, lse_part, delta_part, flat_k, flat_v, visible
            )
            key_total = key_total + jnp.einsum(
                "hqk,qhd->khd", dscore, query_part, preferred_element_type=jnp.float32
            )
            value_total = value_total + jnp.einsum(
                "hqk,qhd->khd", probs_low, grad_part, preferred_element_type=jnp.float32
            )
            return (key_total, value_total)

        return key_block

    query_grad = in_blocks(
        query_block,
        zeros_heads,
        (
            lax.all_gather(flat_k, "blk", axis=0, tiled=True),
            lax.all_gather(flat_v, "blk", axis=0, tiled=True),
        ),
    )
    lse_all, delta_all = (
        lax.all_gather(log_total.T, "blk", axis=0, tiled=True),
        lax.all_gather(row_delta.T, "blk", axis=0, tiled=True),
    )
    key_grad, value_grad = in_blocks(
        key_block_with(lse_all, delta_all),
        (zeros_rows, zeros_rows),
        (
            lax.all_gather(flat_q, "blk", axis=0, tiled=True),
            lax.all_gather(flat_g, "blk", axis=0, tiled=True),
        ),
    )

    def restore(array):
        return array.astype(jnp.bfloat16).reshape(2, span_rows, local_heads * DH)

    query_rows = jnp.transpose(query_grad, (1, 0, 2))
    return (attended_all, restore(query_rows), restore(key_grad), restore(value_grad))


def solution(mesh):
    in_specs = (
        P("blk", None, "head"),
        P("blk", None, "head"),
        P("blk", None, "head"),
        P("blk", None, "head"),
        P(),
    )
    out_specs = (
        P("blk", None, None),
        P("blk", None, "head"),
        P("blk", None, "head"),
        P("blk", None, "head"),
    )
    return jax.shard_map(body, mesh=mesh, in_specs=in_specs, out_specs=out_specs, check_vma=False)
```

profile of v0, /device:TPU:33, one launch (start us, length us, event | category | flops | bytes accessed | tf_op | source)
XLA Modules:
  0.0 541.5 jit_solution(10403152739263997043)
XLA Ops:
  7.2 1.6 reshape.259
  8.9 1.6 reshape.262
  10.6 1.6 reshape.265
  12.2 1.6 reshape.261
  18.5 60.9 %all-gather.6.cloned.1.call-done = bf16[8192,2,128]{2,1,0:T(2,128)(2,1)} async-done(((bf16[256,2,128]{2,1,0:T(2,128)(2,1)}), bf16[8192,2,128]{2,1,0:T(2,128)(2,1)}) %all-gather.6.cloned.1.call-update) | async-done | bytes 4194320 | tf_op jit(solution)/shard_map/all_gather | solution.py:93
  79.4 5.1 copy.104
  84.5 63.8 %all-gather.8.cloned.1.call-done = bf16[8192,2,128]{2,1,0:T(2,128)(2,1)} async-done(((bf16[256,2,128]{2,1,0:T(2,128)(2,1)}), bf16[8192,2,128]{2,1,0:T(2,128)(2,1)}) %all-gather.8.cloned.1.call-update) | async-done | bytes 4194320 | tf_op jit(solution)/shard_map/all_gather | solution.py:94
  148.3 5.2 copy.106
  153.5 92.2 %while.45 = (s32[]{:T(128)}, f32[2,256]{1,0:T(2,128)S(1)}, f32[2,256]{1,0:T(2,128)S(1)}, f32[2,256,128]{2,1,0:T(8,128)S(1)}, s32[16]{0:T(128)S(1)}, /*index=5*/s...) while((s32[]{:T(128)}, f32[2,256]{1,0:T(2,128)S(1)}, ...), condition=%wide.region_5.6_spmd.clone, body=%wide.region_1.5_spmd.clone.sunk | while | flops 472302592 | bytes 4897173 | solution.py:31
  157.2 2.0 convolution_add_fusion.2
  162.9 2.0 convolution_add_fusion.2
  168.7 2.1 convolution_add_fusion.2
  174.5 2.0 convolution_add_fusion.2
  180.2 2.0 convolution_add_fusion.2
  186.0 2.0 convolution_add_fusion.2
  191.8 2.0 convolution_add_fusion.2
  197.5 2.0 convolution_add_fusion.2
  203.3 2.1 convolution_add_fusion.2
  209.0 2.0 convolution_add_fusion.2
  214.8 2.0 convolution_add_fusion.2
  220.6 2.0 convolution_add_fusion.2
  226.3 2.0 convolution_add_fusion.2
  232.1 2.0 convolution_add_fusion.2
  237.8 2.0 convolution_add_fusion.2
  243.6 2.0 convolution_add_fusion.2
  246.6 52.4 %all_gather.29 = f32[8192,2]{1,0:T(8,128)} all-gather(f32[256,2]{1,0:T(8,128)S(1)} %bitcast.135), channel_id=1, replica_groups=mesh['head'=8,'blk'=32] {'blk'}, dimensions={0}, use_global_device_ids=true | all-gather | bytes 67584 | tf_op jit(solution)/shard_map/all_gather | solution.py:159
  299.0 2.8 copy.121
  301.8 33.6 %all_gather.27 = f32[8192,2]{0,1:T(2,128)S(1)} all-gather(f32[256,2]{0,1:T(2,128)S(1)} %bitcast.139), channel_id=1, replica_groups=mesh['head'=8,'blk'=32] {'blk'}, dimensions={0}, use_global_device_ids=true | all-gather | bytes 67584 | tf_op jit(solution)/shard_map/all_gather | solution.py:158
  335.4 110.1 %while.47 = (s32[]{:T(128)}, f32[256,2,128]{0,2,1:T(8,128)S(1)}, f32[256,2,128]{0,2,1:T(8,128)S(1)}, bf16[16,512,2,128]{3,2,1,0:T(2,128)(2,1)}, s32[256]{0:T(256...) while((s32[]{:T(128)}, f32[256,2,128]{0,2,1:T(8,128)S(1)}, ...), condition=%wide.region_12.13_spmd.clone, body=%wide.region_10.12_spmd.clone.sunk | while | flops 271301120 | bytes 6854102 | solution.py:31
  339.6 1.4 constant_dynamic-slice_fusion.3
  446.3 83.8 %while.46 = (s32[]{:T(128)}, f32[2,256,128]{2,1,0:T(8,128)S(1)}, s32[16]{0:T(128)S(1)}, s32[64]{0:T(128)S(1)}, s32[256]{0:T(256)S(1)}, /*index=5*/bf16[16,512,2,...) while((s32[]{:T(128)}, f32[2,256,128]{2,1,0:T(8,128)S(1)}, ...), condition=%wide.region_9.10_spmd.clone, body=%wide.region_7.9_spmd.clone.sunk | while | flops 203799040 | bytes 3951515 | solution.py:31
  449.8 1.7 fusion.114
  455.0 1.7 fusion.114
  460.3 1.7 fusion.114
  465.5 1.7 fusion.114
  470.7 1.7 fusion.114
  476.0 1.7 fusion.114
  481.2 1.7 fusion.114
  486.5 1.7 fusion.114
  491.7 1.7 fusion.114
  496.9 1.7 fusion.114
  502.2 1.7 fusion.114
  507.4 1.7 fusion.114
  512.7 1.7 fusion.114
  517.9 1.7 fusion.114
  523.1 1.7 fusion.114
  528.4 1.7 fusion.114
  532.6 2.3 copy.183
  (460 shorter events, 200.0 us)
Async XLA Ops:
  7.2 72.2 %all-gather.6.cloned.1.call-start = ((), (), s32[]{:S(2)}) async-start(), calls=%async_computation | async-start | bytes 4325376 | tf_op jit(solution)/shard_map/all_gather | solution.py:93
  8.8 139.5 %all-gather.8.cloned.1.call-start = ((), (), s32[]{:S(2)}) async-start(), calls=%async_computation.1 | async-start | bytes 4325376 | tf_op jit(solution)/shard_map/all_gather | solution.py:94
  10.5 324.9 %all-gather.14.cloned.1.call-start = ((), (), s32[]{:S(2)}) async-start(), calls=%async_computation.4 | async-start | bytes 4325376 | tf_op jit(solution)/shard_map/all_gather | solution.py:166
  12.2 323.2 %all-gather.12.cloned.1.call-start = ((), (), s32[]{:S(2)}) async-start(), calls=%async_computation.3 | async-start | bytes 4325376 | tf_op jit(solution)/shard_map/all_gather | solution.py:165
  13.8 518.8 %all-gather.10.cloned.1.call-start = ((), (), s32[]{:S(2)}) async-start(), calls=%async_computation.2 | async-start | bytes 1179648 | tf_op jit(solution)/shard_map/all_gather | solution.py:100
  148.3 5.2 copy-start.1
  153.5 92.3 %copy-start = (bf16[256,2,128]{2,1,0:T(2,128)(2,1)S(1)}, bf16[256,2,128]{2,1,0:T(2,128)(2,1)}, u32[]{:S(2)}) copy-start(bf16[256,2,128]{2,1,0:T(2,128)(2,1)} %reshape.265) | copy-start | bytes 393220
Sparse Core Ops, SparseCore 0:
  10.4 68.9 all-gather.5
  81.8 66.4 all-gather.7
  150.7 66.5 all-gather.13
  219.6 75.3 all-gather.11
  446.4 45.2 all-gather.9
where the time goes:
time: 546 us; the launch traced here: 541 us
  waiting for transfers between devices  125 us (23%)
  matrix products  122 us (22%)
  blocking collectives  86 us (16%)
  local copies, waits for them, and re-layouts  80.8 us (15%)
  other arithmetic  79.8 us (15%)
  loops' own time  34 us (6%)
  between operations  13.9 us (3%)
    all_gather x1, waiting for transfers between devices, body(): lax.all_gather(flat_v, 'blk', axis=0, tiled=True)  63.8 us
    all_gather x1, waiting for transfers between devices, body(): lax.all_gather(flat_k, 'blk', axis=0, tiled=True)  60.9 us
    all_gather x1, blocking collectives, body(): lax.all_gather(row_delta.T, 'blk', axis=0, tiled=True)  52.4 us
    dynamic_slice x64, local copies, waits for them, and re-layouts, in_blocks(): finished, unused = lax.scan(visiting, running, (stacked, starts))  50.5 us
    dot_general x48, matrix products, scores_of(): jnp.einsum('qhd,khd->hqk', query_part, key_part, preferred_element_type=j...  49 us
    another operation x3, loops' own time, in_blocks(): finished, unused = lax.scan(visiting, running, (stacked, starts))  34 us
    all_gather x1, blocking collectives, body(): lax.all_gather(log_total.T, 'blk', axis=0, tiled=True)  33.6 us
    dot_general x16, matrix products, attend_block(): jnp.einsum('hqk,khd->hqd', probs, value_part.astype(jnp.float32), preferr...  32.7 us
  transfers between devices with their start and end apart: 5, of which 2 were waited for; matrix products, arithmetic and copies ran while one was open for 37% of the time, Pallas kernels for 0%

commit v1 on v0

v1 whole, which is shorter than its diff:
```python
import functools
import math

import jax
import jax.numpy as jnp
from jax import lax
from jax.experimental import pallas as pl
from jax.experimental.pallas import tpu as pltpu
from jax.sharding import PartitionSpec as P

MESH = pl.DeviceIdType.MESH
DH = 128
SPAN = 128
ROWS = 256
CHUNK = 512
WIDE = 2048
SCALE = DH**-0.5
SCALE2 = DH**-0.5 * math.log2(math.e)
LOW = -1e30
F32 = jnp.float32
BF16 = jnp.bfloat16
NN = (((1,), (0,)), ((), ()))
NT = (((1,), (1,)), ((), ()))
TK, TQ, TV, TG = 0, 1, 2, 3
RO, RV, RK, RQ = 0, 1, 2, 3


def dot(a, b, dims):
    return lax.dot_general(a, b, dims, preferred_element_type=F32)


def kernel(
    order, q_in, k_in, v_in, g_in,
    att_out, dq_out, dk_out, dv_out,
    gathered, probs, qpos, chunk_max, chunk_sum, stat_out, stat_in, delta_out, delta_in, factor,
    turned, key_total, value_held, out_held, query_held,
    staged, from_a_mid, from_a, from_b, from_own,
    g_send, g_recv, r_send, r_recv, s_send, s_recv, d_send, d_recv, h_send, h_recv,
):
    blk = lax.axis_index("blk")
    head = lax.axis_index("head")
    core = blk % 2
    z = (blk // 2) % 8
    x = blk // 16
    odd = z % 2
    other = 1 - core
    y = head % 4
    xh = head // 4

    def at(xx, zz):
        return xx * 16 + zz * 2

    zq = z + 1 - 2 * odd
    zka = (z + 2 * odd + 7) % 8
    zkb = (z + 11 - 6 * odd) % 8
    zkab = (zkb + 2 * (1 - odd) + 7) % 8
    q_a, q_b, q_ab = at(1 - x, z), at(x, zq), at(1 - x, zq)
    k_a, k_b = at(x, zka), at(x, zkb)
    own = at(x, z)
    near_a = {TK: k_a, TV: k_a, TQ: q_a, TG: q_a}
    near_b = {TK: k_b, TV: k_b, TQ: q_b, TG: q_b}
    inputs = {TK: k_in, TV: v_in, TQ: q_in, TG: g_in}

    barrier = pltpu.get_barrier_semaphore()
    chips = (q_a, q_b, q_ab, k_a, k_b)
    for chip in chips:
        for r in range(2):
            pl.semaphore_signal(barrier, inc=1, device_id={"blk": chip + r}, device_id_type=MESH)
    pl.semaphore_signal(barrier, inc=1, device_id={"blk": own + other}, device_id_type=MESH)
    heads_y = [xh * 4 + (y + n) % 4 for n in (1, 2, 3)]
    head_x = (1 - xh) * 4 + y
    for target in heads_y + [head_x]:
        pl.semaphore_signal(barrier, inc=1, device_id={"head": target}, device_id_type=MESH)
    pl.semaphore_wait(barrier, 2 * len(chips) + 1 + 4)

    started = []

    def remote(src, dst, send, recv, axis, device):
        copy = pltpu.make_async_remote_copy(
            src_ref=src, dst_ref=dst, send_sem=send, recv_sem=recv,
            device_id={axis: device}, device_id_type=MESH,
        )
        copy.start()
        started.append(copy)

    def lanes(h):
        return pl.ds(pl.multiple_of(h * DH, DH), DH)

    def rows(r):
        return pl.ds(pl.multiple_of(r * ROWS, ROWS), ROWS)

    def send_b(t):
        for h in range(2):
            remote(inputs[t].at[:, lanes(h)], gathered.at[t, 2, rows(core)],
                   g_send.at[t, h], g_recv.at[t, 4 + core], "blk", near_b[t] + h)

    def send_a(t):
        for h in range(2):
            remote(inputs[t].at[:, lanes(h)], gathered.at[t, 1, rows(core)],
                   g_send.at[t, 2 + h], g_recv.at[t, 2 + core], "blk", near_a[t] + h)

    local = {}

    def send_own(t):
        remote(inputs[t].at[:, lanes(other)], gathered.at[t, 0, rows(core)],
               g_send.at[t, 4], g_recv.at[t, 0], "blk", own + other)
        local[t] = pltpu.make_async_copy(
            inputs[t].at[:, lanes(core)], gathered.at[t, 0, rows(core)], g_recv.at[t, 1])
        local[t].start()

    def arrived(dst, sem):
        pltpu.make_async_remote_copy(
            src_ref=dst, dst_ref=dst, send_sem=sem, recv_sem=sem,
            device_id={"blk": own + other}, device_id_type=MESH,
        ).wait_recv()

    def wait_own(t):
        local[t].wait()
        arrived(gathered.at[t, 0, rows(other)], g_recv.at[t, 0])

    def wait_slot(t, slot):
        for r in range(2):
            arrived(gathered.at[t, slot, pl.ds(r * ROWS, ROWS)], g_recv.at[t, slot * 2 + r])

    def wait_forward(t):
        for r in range(2):
            piece = pl.ds(r * ROWS, ROWS)
            arrived(gathered.at[t, 2, piece], g_recv.at[t, 4 + r])
            remote(gathered.at[t, 2, piece], gathered.at[t, 3, piece],
                   g_send.at[t, 5 + r], g_recv.at[t, 6 + r], "blk", near_a[t] + core)

    for t in (TK, TQ):
        send_b(t)
    for t in (TK, TQ):
        send_own(t)
        send_a(t)
    for t in (TV, TG):
        send_b(t)
    for t in (TV, TG):
        send_a(t)
        send_own(t)

    lane = lax.broadcasted_iota(jnp.int32, (1, SPAN), 1)
    for s, (xx, zz) in enumerate(((x, z), (1 - x, z), (x, zq), (1 - x, zq))):
        for n in range(4):
            first = order[4 * (xx * 8 + zz) + n] * SPAN
            qpos[:, pl.ds(s * CHUNK + n * SPAN, SPAN)] = first + lane
    key_z = (z, zka, zkb, zkab)
    down = lax.broadcasted_iota(jnp.int32, (SPAN, CHUNK), 0)

    def cols(i):
        return pl.ds(i * CHUNK, CHUNK)

    def score_tile(j, i):
        s = dot(gathered[TK, j], gathered[TQ, i], NT)
        place = qpos[:, cols(i)]
        parts = []
        for n in range(4):
            first = order[4 * (x * 8 + key_z[j]) + n] * SPAN
            parts.append(jnp.where(down <= place - first, s[n * SPAN:(n + 1) * SPAN], LOW))
        s = jnp.concatenate(parts, axis=0)
        top = jnp.max(s, axis=0, keepdims=True)
        p = jnp.exp2((s - top) * SCALE2)
        chunk_sum[j:j + 1, cols(i)] = jnp.sum(p, axis=0, keepdims=True)
        chunk_max[j:j + 1, cols(i)] = top
        probs[j, :, cols(i)] = p.astype(BF16)

    wait_own(TK)
    wait_own(TQ)
    score_tile(0, 0)
    wait_slot(TQ, 1)
    score_tile(0, 1)
    wait_forward(TQ)
    score_tile(0, 2)
    wait_slot(TK, 1)
    score_tile(1, 0)
    score_tile(1, 1)
    wait_forward(TK)
    score_tile(1, 2)
    score_tile(2, 0)
    score_tile(2, 1)
    score_tile(2, 2)
    wait_slot(TQ, 3)
    score_tile(0, 3)
    score_tile(1, 3)
    score_tile(2, 3)
    wait_forward(TG)
    wait_slot(TK, 3)
    for i in range(4):
        score_tile(3, i)

    peers = (q_a, q_b, q_ab)
    tops = [chunk_max[j:j + 1, :] for j in range(4)]
    sums = [chunk_sum[j:j + 1, :] for j in range(4)]
    top = functools.reduce(jnp.maximum, tops)
    total = sum(s * jnp.exp2((m - top) * SCALE2) for s, m in zip(sums, tops))
    stat_out[0:1, :] = top
    stat_out[1:2, :] = total
    for n, peer in enumerate(peers):
        remote(stat_out, stat_in.at[n], s_send.at[n], s_recv.at[n], "blk", peer + core)
    wait_forward(TV)

    def turned_row(ref_row, n):
        return jnp.concatenate([ref_row[:, cols(s ^ (n + 1))] for s in range(4)], axis=1)

    wait_own(TV)
    wait_own(TG)
    wait_slot(TV, 1)
    wait_slot(TG, 1)
    all_tops, all_sums = [top], [total]
    for n in range(3):
        arrived(stat_in.at[n], s_recv.at[n])
        all_tops.append(turned_row(stat_in.at[n, pl.ds(0, 1)], n))
        all_sums.append(turned_row(stat_in.at[n, pl.ds(1, 1)], n))
    whole_top = functools.reduce(jnp.maximum, all_tops)
    whole_sum = sum(s * jnp.exp2((m - whole_top) * SCALE2) for s, m in zip(all_sums, all_tops))
    inverse = 1.0 / whole_sum
    for j in range(4):
        factor[j:j + 1, :] = jnp.exp2((tops[j] - whole_top) * SCALE2) * inverse

    def weigh(j, i):
        p = probs[j, :, cols(i)] * factor[j:j + 1, cols(i)].astype(BF16)
        probs[j, :, cols(i)] = p
        return dot(gathered[TV, j].T, p, NN)

    for i in range(4):
        turned[:, cols(i)] = weigh(0, i) + weigh(1, i) + weigh(2, i)
    wait_slot(TG, 3)
    wait_slot(TV, 3)

    red_a = {RO: q_a, RQ: q_a, RK: k_a, RV: k_a}
    red_b = {RO: q_b, RQ: q_b, RK: k_b, RV: k_b}

    def reduce_ab(t, part):
        staged[t, 3] = part.astype(BF16)
        remote(staged.at[t, 3], from_a_mid.at[t], r_send.at[t, 0], r_recv.at[t, 0], "blk", red_a[t] + core)

    def reduce_b(t, part):
        arrived(from_a_mid.at[t], r_recv.at[t, 0])
        staged[t, 2] = (part + from_a_mid[t].astype(F32)).astype(BF16)
        for r in range(2):
            remote(staged.at[t, 2, pl.ds(r * ROWS, ROWS)], from_b.at[t, core],
                   r_send.at[t, 1 + r], r_recv.at[t, 1 + core], "blk", red_b[t] + r)

    def reduce_a(t, part):
        staged[t, 1] = part.astype(BF16)
        for r in range(2):
            remote(staged.at[t, 1, pl.ds(r * ROWS, ROWS)], from_a.at[t, core],
                   r_send.at[t, 3 + r], r_recv.at[t, 3 + core], "blk", red_a[t] + r)

    def reduce_own(t, part):
        staged[t, 0] = part.astype(BF16)
        remote(staged.at[t, 0, rows(other)], from_own.at[t, core],
               r_send.at[t, 5], r_recv.at[t, 5], "blk", own + other)
        from_own[t, core] = staged[t, 0, rows(core)]

    def reduced(t):
        arrived(from_own.at[t, other], r_recv.at[t, 5])
        for h in range(2):
            arrived(from_a.at[t, h], r_recv.at[t, 3 + h])
            arrived(from_b.at[t, h], r_recv.at[t, 1 + h])
        return [
            (from_own[t, h].astype(F32) + from_a[t, h].astype(F32) + from_b[t, h].astype(F32)).astype(BF16)
            for h in range(2)
        ]

    for i in (3, 2, 1, 0):
        o = turned[:, cols(i)] + weigh(3, i)
        delta_out[:, cols(i)] = jnp.sum(o * gathered[TG, i].astype(F32).T, axis=0, keepdims=True)
        o = o.T
        if i == 3:
            reduce_ab(RO, o)
        elif i == 2:
            out_held[...] = o
        elif i == 1:
            reduce_a(RO, o)
        else:
            reduce_own(RO, o)
    for n, peer in enumerate(peers):
        remote(delta_out, delta_in.at[n], d_send.at[n], d_recv.at[n], "blk", peer + core)

    for j in (3, 2, 1, 0):
        part = sum(dot(probs[j, :, cols(i)], gathered[TG, i], NN) for i in range(4))
        if j == 3:
            reduce_ab(RV, part)
        elif j == 2:
            value_held[...] = part
        elif j == 1:
            reduce_a(RV, part)
        else:
            reduce_own(RV, part)

    delta = delta_out[...]
    for n in range(3):
        arrived(delta_in.at[n], d_recv.at[n])
        delta = delta + turned_row(delta_in.at[n], n)
    delta_out_rows = [delta[:, i * CHUNK:(i + 1) * CHUNK] for i in range(4)]

    fresh_k, fresh_q = set(), set()

    def grad_tile(j, i):
        dp = dot(gathered[TV, j], gathered[TG, i], NT)
        ds = (probs[j, :, cols(i)].astype(F32) * (dp - delta_out_rows[i])).astype(BF16)
        key_part = dot(ds, gathered[TQ, i], NN)
        query_part = dot(gathered[TK, j].T, ds, NN)
        if j in fresh_k:
            key_total[j] += key_part
        else:
            key_total[j] = key_part
        if i in fresh_q:
            turned[:, cols(i)] += query_part
        else:
            turned[:, cols(i)] = query_part
        fresh_k.add(j)
        fresh_q.add(i)

    def key_part_of(j):
        return key_total[j] * SCALE

    def query_part_of(i):
        return turned[:, cols(i)].T * SCALE

    for i in range(4):
        grad_tile(3, i)
    reduce_ab(RK, key_part_of(3))
    for j in range(3):
        grad_tile(j, 3)
    reduce_ab(RQ, query_part_of(3))
    reduce_b(RO, out_held[...])
    reduce_b(RV, value_held[...])
    for i in range(3):
        grad_tile(2, i)
    for j in range(2):
        grad_tile(j, 2)
    reduce_b(RK, key_part_of(2))
    reduce_b(RQ, query_part_of(2))
    for j in (1, 0):
        for i in (1, 0):
            grad_tile(j, i)
    reduce_a(RK, key_part_of(1))
    reduce_a(RQ, query_part_of(1))
    reduce_own(RK, key_part_of(0))
    reduce_own(RQ, query_part_of(0))

    def block_of(h):
        return pl.ds(pl.multiple_of(h * 2 * DH, 2 * DH), 2 * DH)

    mine = reduced(RO)
    att_out[:, block_of(head)] = jnp.concatenate(mine, axis=1)

    def share(source, base, targets):
        for n, target in enumerate(targets):
            remote(att_out.at[:, block_of(source)], att_out.at[:, block_of(source)],
                   h_send.at[base + n], h_recv.at[source], "head", target)

    def wait_share(source):
        arrived(att_out.at[:, block_of(source)], h_recv.at[source])

    share(head, 0, [head_x] + heads_y)

    value = reduced(RV)
    for h in range(2):
        dv_out[:, h * DH:(h + 1) * DH] = value[h]

    wait_share(head_x)
    share(head_x, 4, heads_y)

    for t, out in ((RK, dk_out), (RQ, dq_out)):
        part = reduced(t)
        for h in range(2):
            out[:, h * DH:(h + 1) * DH] = part[h]
    for n in (1, 2, 3):
        wait_share(xh * 4 + (y + n) % 4)
        wait_share((1 - xh) * 4 + (y + n) % 4)
    for copy in started:
        copy.wait_send()


def body(queries, key_vectors, value_vectors, out_grad, block_order):
    def flat(array):
        return array.reshape(ROWS, 2 * DH)

    vmem = pl.BlockSpec(memory_space=pltpu.VMEM)
    dma = pltpu.SemaphoreType.DMA
    small = jax.ShapeDtypeStruct((ROWS, 2 * DH), BF16)
    outs = pl.pallas_call(
        kernel,
        out_shape=(jax.ShapeDtypeStruct((ROWS, 16 * DH), BF16), small, small, small),
        in_specs=[pl.BlockSpec(memory_space=pltpu.SMEM)] + [vmem] * 4,
        out_specs=(vmem,) * 4,
        scratch_shapes=[
            pltpu.VMEM((4, 4, CHUNK, DH), BF16),
            pltpu.VMEM((4, CHUNK, WIDE), BF16),
            pltpu.VMEM((1, WIDE), jnp.int32),
            pltpu.VMEM((4, WIDE), F32),
            pltpu.VMEM((4, WIDE), F32),
            pltpu.VMEM((2, WIDE), F32),
            pltpu.VMEM((3, 2, WIDE), F32),
            pltpu.VMEM((1, WIDE), F32),
            pltpu.VMEM((3, 1, WIDE), F32),
            pltpu.VMEM((4, WIDE), F32),
            pltpu.VMEM((DH, WIDE), F32),
            pltpu.VMEM((4, CHUNK, DH), F32),
            pltpu.VMEM((CHUNK, DH), F32),
            pltpu.VMEM((CHUNK, DH), F32),
            pltpu.VMEM((CHUNK, DH), F32),
            pltpu.VMEM((4, 4, CHUNK, DH), BF16),
            pltpu.VMEM((4, CHUNK, DH), BF16),
            pltpu.VMEM((4, 2, ROWS, DH), BF16),
            pltpu.VMEM((4, 2, ROWS, DH), BF16),
            pltpu.VMEM((4, 2, ROWS, DH), BF16),
            dma((4, 7)), dma((4, 8)),
            dma((4, 6)), dma((4, 6)),
            dma((3,)), dma((3,)),
            dma((3,)), dma((3,)),
            dma((7,)), dma((8,)),
        ],
        compiler_params=pltpu.CompilerParams(
            collective_id=0, has_side_effects=True, vmem_limit_bytes=56 << 20
        ),
        cost_estimate=pl.CostEstimate(
            flops=12 * WIDE * WIDE * DH, bytes_accessed=3 << 20, transcendentals=WIDE * WIDE
        ),
    )(block_order, flat(queries), flat(key_vectors), flat(value_vectors), flat(out_grad))
    attended, query_grad, key_grad, value_grad = outs
    return (
        attended.reshape(2, SPAN, 16 * DH),
        query_grad.reshape(2, SPAN, 2 * DH),
        key_grad.reshape(2, SPAN, 2 * DH),
        value_grad.reshape(2, SPAN, 2 * DH),
    )


def solution(mesh):
    split = P("blk", None, "head")
    return jax.shard_map(
        body,
        mesh=mesh,
        in_specs=(split, split, split, split, P()),
        out_specs=(P("blk", None, None), split, split, split),
        check_vma=False,
    )
```

time: 546 us -> 76.5 us (0.14)
  the two profiles are of different devices: /device:TPU:33 before, /device:TPU:5 now
where the time goes in v1:
time: 76.5 us; the launch traced here: 76.3 us
  Pallas kernels  70.7 us (92%)
  local copies, waits for them, and re-layouts  4.9 us (6%)
    pallas_call x1, Pallas kernels, body(): pl.pallas_call(kernel, out_shape=(jax.ShapeDtypeStruct((ROWS, 16 * DH), B...  70.7 us
    unnamed x10, local copies, waits for them, and re-layouts  4.9 us

profile of v1, /device:TPU:5, one launch (start us, length us, event | category | flops | bytes accessed | tf_op | source)
XLA Modules:
  0.0 76.3 jit_solution(15590329427200171246)
XLA Ops:
  0.6 70.7 %shard_map.84 = (bf16[256,2048]{1,0:T(8,128)(2,1)}, bf16[256,256]{1,0:T(8,128)(2,1)}, bf16[256,256]{1,0:T(8,128)(2,1)}, bf16[256,256]{1,0:T(8,128)(2,1)}) custom-call(s32[64]{0:T(128)} %order.1, bf16[256,256]{1,0:T(8,128)(2,1)} %bitcast.12, bf16[256,256]{1,0:T(8,128)(2,1)} %bitcast.13, bf16[256,256]{1,0:T(8,128)(2,1)} %bitcast.14, bf16[256,256]{1,0:T(8,128)(2,1)} %bitcast.15), custom_call_target="tpu_custom_call" | custom-call | flops 6442450944 | bytes 3145728 | tf_op jit(solution)/shard_map/pallas_call | solution.py:386
  71.4 0.0 copy-start.2
  71.4 2.3 %copy.13 = bf16[2,128,2048]{2,1,0:T(8,128)(2,1)} copy(bf16[2,128,2048]{2,1,0:T(8,128)(2,1)} %bitcast.8) | data formatting | bytes 2097152
  73.7 0.0 copy-done.2
  73.7 0.0 copy-start.1
  73.7 0.7 copy.14
  74.4 0.3 copy-done.1
  74.7 0.0 copy-start
  74.7 0.7 copy.15
  75.3 0.3 copy-done
  75.6 0.7 copy.16
Async XLA Ops:
  71.4 2.4 %copy-start.2 = (bf16[256,256]{1,0:T(8,128)(2,1)S(1)}, bf16[256,256]{1,0:T(8,128)(2,1)}, u32[]{:S(2)}) copy-start(bf16[256,256]{1,0:T(8,128)(2,1)} %get-tuple-element.9) | copy-start | bytes 393220
  73.7 1.0 %copy-start.1 = (bf16[256,256]{1,0:T(8,128)(2,1)S(1)}, bf16[256,256]{1,0:T(8,128)(2,1)}, u32[]{:S(2)}) copy-start(bf16[256,256]{1,0:T(8,128)(2,1)} %get-tuple-element.10) | copy-start | bytes 393220
  74.7 1.0 %copy-start = (bf16[256,256]{1,0:T(8,128)(2,1)S(1)}, bf16[256,256]{1,0:T(8,128)(2,1)}, u32[]{:S(2)}) copy-start(bf16[256,256]{1,0:T(8,128)(2,1)} %get-tuple-element.11) | copy-start | bytes 393220

commit v2 on v1

v2 whole, which is shorter than its diff:
```python
import functools
import math

import jax
import jax.numpy as jnp
from jax import lax
from jax.experimental import pallas as pl
from jax.experimental.pallas import tpu as pltpu
from jax.sharding import PartitionSpec as P

MESH = pl.DeviceIdType.MESH
DH = 128
SPAN = 128
ROWS = 256
CHUNK = 512
WIDE = 2048
SCALE = DH**-0.5
SCALE2 = DH**-0.5 * math.log2(math.e)
LOW = -1e30
F32 = jnp.float32
BF16 = jnp.bfloat16
NN = (((1,), (0,)), ((), ()))
NT = (((1,), (1,)), ((), ()))
TK, TQ, TV, TG = 0, 1, 2, 3
RO, RV, RK, RQ = 0, 1, 2, 3


def dot(a, b, dims):
    return lax.dot_general(a, b, dims, preferred_element_type=F32)


def kernel(
    order, q_in, k_in, v_in, g_in,
    att_out, dq_out, dk_out, dv_out,
    gathered, probs, dprobs, qpos, chunk_max, chunk_sum, stat_out, stat_in, delta_out, delta_in, factor,
    turned, key_total, value_held, key_held, query_held,
    staged, from_a_mid, from_a, from_b, from_own, from_ab,
    g_send, g_recv, r_send, r_recv, s_send, s_recv, d_send, d_recv, h_send, h_recv,
):
    blk = lax.axis_index("blk")
    head = lax.axis_index("head")
    core = blk % 2
    z = (blk // 2) % 8
    x = blk // 16
    odd = z % 2
    other = 1 - core
    y = head % 4
    xh = head // 4

    def at(xx, zz):
        return xx * 16 + zz * 2

    zq = z + 1 - 2 * odd
    zka = (z + 2 * odd + 7) % 8
    zkb = (z + 11 - 6 * odd) % 8
    zkab = (zkb + 2 * (1 - odd) + 7) % 8
    q_a, q_b, q_ab = at(1 - x, z), at(x, zq), at(1 - x, zq)
    k_a, k_b = at(x, zka), at(x, zkb)
    own = at(x, z)
    near_a = {TK: k_a, TV: k_a, TQ: q_a, TG: q_a}
    near_b = {TK: k_b, TV: k_b, TQ: q_b, TG: q_b}
    inputs = {TK: k_in, TV: v_in, TQ: q_in, TG: g_in}

    barrier = pltpu.get_barrier_semaphore()
    chips = (q_a, q_b, q_ab, k_a, k_b)
    for chip in chips:
        for r in range(2):
            pl.semaphore_signal(barrier, inc=1, device_id={"blk": chip + r}, device_id_type=MESH)
    pl.semaphore_signal(barrier, inc=1, device_id={"blk": own + other}, device_id_type=MESH)
    heads_y = [xh * 4 + (y + n) % 4 for n in (1, 2, 3)]
    head_x = (1 - xh) * 4 + y
    for target in heads_y + [head_x]:
        pl.semaphore_signal(barrier, inc=1, device_id={"head": target}, device_id_type=MESH)

    def lanes(h):
        return pl.ds(pl.multiple_of(h * DH, DH), DH)

    def rows(r):
        return pl.ds(pl.multiple_of(r * ROWS, ROWS), ROWS)

    def cols(i):
        return pl.ds(i * CHUNK, CHUNK)

    halves = (pl.ds(0, ROWS), pl.ds(ROWS, ROWS))

    local = {}
    for t in (TK, TQ, TV, TG):
        local[t] = pltpu.make_async_copy(
            inputs[t].at[:, lanes(core)], gathered.at[t, 0, rows(core)], g_recv.at[t, 1])
        local[t].start()
    lane = lax.broadcasted_iota(jnp.int32, (1, SPAN), 1)
    for s, (xx, zz) in enumerate(((x, z), (1 - x, z), (x, zq), (1 - x, zq))):
        for n in range(4):
            first = order[4 * (xx * 8 + zz) + n] * SPAN
            qpos[:, pl.ds(s * CHUNK + n * SPAN, SPAN)] = first + lane
    pl.semaphore_wait(barrier, 2 * len(chips) + 1 + 4)

    started = []

    def remote(src, dst, send, recv, axis, device):
        copy = pltpu.make_async_remote_copy(
            src_ref=src, dst_ref=dst, send_sem=send, recv_sem=recv,
            device_id={axis: device}, device_id_type=MESH,
        )
        copy.start()
        started.append(copy)

    PIECES = 2
    PIECE = ROWS // PIECES

    def piece_of(r, n):
        return pl.ds(pl.multiple_of(r * ROWS + n * PIECE, PIECE), PIECE)

    def send_to(t, slot, chip, ns):
        for n in ns:
            for h in range(2):
                remote(inputs[t].at[pl.ds(n * PIECE, PIECE), lanes(h)], gathered.at[t, slot, piece_of(core, n)],
                       g_send.at[t, (slot * 2 + h) * PIECES + n], g_recv.at[t, (slot * 2 + core) * PIECES + n],
                       "blk", chip + h)

    def send_b(t, ns=range(PIECES)):
        send_to(t, 2, near_b[t], ns)

    def send_a(t, ns=range(PIECES)):
        send_to(t, 1, near_a[t], ns)

    def send_own(t):
        remote(inputs[t].at[:, lanes(other)], gathered.at[t, 0, rows(core)],
               g_send.at[t, 0], g_recv.at[t, 0], "blk", own + other)

    def arrived(dst, sem):
        pltpu.make_async_remote_copy(
            src_ref=dst, dst_ref=dst, send_sem=sem, recv_sem=sem,
            device_id={"blk": own + other}, device_id_type=MESH,
        ).wait_recv()

    def wait_own(t):
        local[t].wait()
        arrived(gathered.at[t, 0, rows(other)], g_recv.at[t, 0])

    def wait_slot(t, slot):
        for n in range(PIECES):
            for r in range(2):
                arrived(gathered.at[t, slot, piece_of(r, n)], g_recv.at[t, (slot * 2 + r) * PIECES + n])

    def wait_forward(t, ns=range(PIECES)):
        for n in ns:
            for r in range(2):
                arrived(gathered.at[t, 2, piece_of(r, n)], g_recv.at[t, (4 + r) * PIECES + n])
                remote(gathered.at[t, 2, piece_of(r, n)], gathered.at[t, 3, piece_of(r, n)],
                       g_send.at[t, (6 + r) * PIECES + n], g_recv.at[t, (6 + r) * PIECES + n], "blk", near_a[t] + core)

    key_z = (z, zka, zkb, zkab)
    down = lax.broadcasted_iota(jnp.int32, (SPAN, CHUNK), 0)

    def score_tile(j, i):
        s = dot(gathered[TK, j], gathered[TQ, i], NT)
        place = qpos[:, cols(i)]
        parts = []
        for n in range(4):
            first = order[4 * (x * 8 + key_z[j]) + n] * SPAN
            parts.append(jnp.where(down <= place - first, s[n * SPAN:(n + 1) * SPAN], LOW))
        s = jnp.concatenate(parts, axis=0)
        top = jnp.max(s, axis=0, keepdims=True)
        p = jnp.exp2((s - top) * SCALE2)
        chunk_sum[j:j + 1, cols(i)] = jnp.sum(p, axis=0, keepdims=True)
        chunk_max[j:j + 1, cols(i)] = top
        probs[j, :, cols(i)] = p.astype(BF16)

    def dprob_tile(j, i):
        dprobs[j, :, cols(i)] = dot(gathered[TV, j], gathered[TG, i], NT)

    for t in (TK, TQ, TG, TV):
        send_b(t)
    for t in (TK, TQ, TG, TV):
        send_a(t)
    for t in (TK, TQ, TG, TV):
        send_own(t)

    def scores(*tiles):
        for j, i in tiles:
            score_tile(j, i)

    wait_own(TK)
    wait_own(TQ)
    scores((0, 0))
    wait_slot(TQ, 1)
    scores((0, 1))
    wait_slot(TK, 1)
    scores((1, 0), (1, 1))
    wait_forward(TK)
    scores((2, 0), (2, 1))
    wait_forward(TQ)
    scores((0, 2), (1, 2), (2, 2))
    wait_slot(TK, 3)
    scores((3, 0), (3, 1), (3, 2))
    wait_slot(TQ, 3)
    scores((0, 3), (1, 3))
    wait_forward(TG)
    scores((2, 3), (3, 3))

    peers = (q_a, q_b, q_ab)
    tops = [chunk_max[j:j + 1, :] for j in range(4)]
    sums = [chunk_sum[j:j + 1, :] for j in range(4)]
    top = functools.reduce(jnp.maximum, tops)
    total = sum(s * jnp.exp2((m - top) * SCALE2) for s, m in zip(sums, tops))
    stat_out[0:1, :] = top
    stat_out[1:2, :] = total
    for n, peer in enumerate(peers):
        remote(stat_out, stat_in.at[n], s_send.at[n], s_recv.at[n], "blk", peer + core)

    def turned_row(ref_row, n):
        return jnp.concatenate([ref_row[:, cols(s ^ (n + 1))] for s in range(4)], axis=1)

    wait_forward(TV)
    wait_own(TV)
    wait_own(TG)
    wait_slot(TV, 1)
    wait_slot(TG, 1)
    for i in range(3):
        dprob_tile(0, i)
        dprob_tile(1, i)
    all_tops, all_sums = [top], [total]
    for n in range(3):
        arrived(stat_in.at[n], s_recv.at[n])
        all_tops.append(turned_row(stat_in.at[n, pl.ds(0, 1)], n))
        all_sums.append(turned_row(stat_in.at[n, pl.ds(1, 1)], n))
    whole_top = functools.reduce(jnp.maximum, all_tops)
    whole_sum = sum(s * jnp.exp2((m - whole_top) * SCALE2) for s, m in zip(all_sums, all_tops))
    inverse = 1.0 / whole_sum
    for j in range(4):
        factor[j:j + 1, :] = jnp.exp2((tops[j] - whole_top) * SCALE2) * inverse

    red_a = {RO: q_a, RQ: q_a, RK: k_a, RV: k_a}
    red_b = {RO: q_b, RQ: q_b, RK: k_b, RV: k_b}

    def reduce_ab(t, part, r):
        staged[t, 3, halves[r]] = part.astype(BF16)
        remote(staged.at[t, 3, halves[r]], from_a_mid.at[t, halves[r]],
               r_send.at[t, 6 + r], r_recv.at[t, 6 + r], "blk", red_a[t] + core)

    def reduce_b(t, held):
        for r in range(2):
            arrived(from_a_mid.at[t, halves[r]], r_recv.at[t, 6 + r])
            staged[t, 2, halves[r]] = (held[halves[r]] + from_a_mid[t, halves[r]].astype(F32)).astype(BF16)
            remote(staged.at[t, 2, halves[r]], from_b.at[t, core],
                   r_send.at[t, 1 + r], r_recv.at[t, 1 + core], "blk", red_b[t] + r)

    def reduce_straight(t, slot, part, chip, into, at_sem):
        staged[t, slot] = part.astype(BF16)
        for r in range(2):
            remote(staged.at[t, slot, halves[r]], into.at[t, core],
                   r_send.at[t, at_sem + r], r_recv.at[t, at_sem + core], "blk", chip + r)

    def reduce_a(t, part):
        reduce_straight(t, 1, part, red_a[t], from_a, 3)

    def reduce_own(t, part):
        staged[t, 0] = part.astype(BF16)
        remote(staged.at[t, 0, rows(other)], from_own.at[t, core],
               r_send.at[t, 5], r_recv.at[t, 5], "blk", own + other)
        from_own[t, core] = staged[t, 0, rows(core)]

    def reduced(t):
        arrived(from_own.at[t, other], r_recv.at[t, 5])
        for h in range(2):
            arrived(from_a.at[t, h], r_recv.at[t, 3 + h])
            arrived(from_b.at[t, h], r_recv.at[t, 1 + h])
        return [
            from_own[t, h].astype(F32) + from_a[t, h].astype(F32) + from_b[t, h].astype(F32)
            for h in range(2)
        ]

    def weigh_tile(j, i):
        p = probs[j, :, cols(i)] * factor[j:j + 1, cols(i)].astype(BF16)
        probs[j, :, cols(i)] = p
        return dot(gathered[TV, j].T, p, NN) if j < 3 else None

    for i in range(4):
        weigh_tile(3, i)
    wait_slot(TG, 3)

    def value_part(j):
        part = None
        for i in range(4):
            term = dot(probs[j, :, cols(i)], gathered[TG, i], NN)
            part = term if part is None else part + term
        return part

    part = value_part(3)
    for r in range(2):
        reduce_ab(RV, part[r * ROWS:(r + 1) * ROWS], r)
    for i in range(4):
        turned[:, cols(i)] = weigh_tile(0, i) + weigh_tile(1, i) + weigh_tile(2, i)
    reduce_a(RV, value_part(1))
    wait_slot(TV, 3)
    for i in range(4):
        o = turned[:, cols(i)] + dot(gathered[TV, 3].T, probs[3, :, cols(i)], NN)
        turned[:, cols(i)] = o
        delta_out[:, cols(i)] = jnp.sum(o * gathered[TG, i].astype(F32).T, axis=0, keepdims=True)
    for n, peer in enumerate(peers):
        remote(delta_out, delta_in.at[n], d_send.at[n], d_recv.at[n], "blk", peer + core)

    for i in (3, 2, 1, 0):
        o = turned[:, cols(i)].T
        if i == 3:
            reduce_straight(RO, 3, o, q_ab, from_ab, 6)
        elif i == 2:
            reduce_straight(RO, 2, o, q_b, from_b, 1)
        elif i == 1:
            reduce_a(RO, o)
        else:
            reduce_own(RO, o)
    value_held[...] = value_part(2)
    reduce_own(RV, value_part(0))

    for j, i in [(3, 0), (3, 1), (3, 2), (3, 3), (0, 3), (1, 3), (2, 3), (2, 0), (2, 1), (2, 2)]:
        dprob_tile(j, i)

    delta = delta_out[...]
    for n in range(3):
        arrived(delta_in.at[n], d_recv.at[n])
        delta = delta + turned_row(delta_in.at[n], n)
    delta_rows = [delta[:, i * CHUNK:(i + 1) * CHUNK] for i in range(4)]

    fresh_q = set()

    def grad_tile(j, i, part=pl.ds(0, CHUNK)):
        ds = (probs[j, part, cols(i)].astype(F32) * (dprobs[j, part, cols(i)] - delta_rows[i])).astype(BF16)
        query_part = dot(gathered[TK, j, part].T, ds, NN)
        if i in fresh_q:
            turned[:, cols(i)] += query_part
        else:
            turned[:, cols(i)] = query_part
        fresh_q.add(i)
        return dot(ds, gathered[TQ, i], NN)

    def query_part_of(i):
        return turned[:, cols(i)].T * SCALE

    for r in range(2):
        part = sum(grad_tile(3, i, halves[r]) for i in range(4))
        reduce_ab(RK, part * SCALE, r)
    for j in range(3):
        key_total[j] = grad_tile(j, 3)
    part = query_part_of(3)
    for r in range(2):
        reduce_ab(RQ, part[r * ROWS:(r + 1) * ROWS], r)
    key_held[...] = (key_total[2] + sum(grad_tile(2, i) for i in range(3))) * SCALE
    reduce_b(RV, value_held)
    for j in range(2):
        key_total[j] += grad_tile(j, 2)
    query_held[...] = query_part_of(2)
    reduce_a(RK, (key_total[1] + sum(grad_tile(1, i) for i in range(2))) * SCALE)
    reduce_own(RK, (key_total[0] + sum(grad_tile(0, i) for i in range(2))) * SCALE)
    reduce_a(RQ, query_part_of(1))
    reduce_own(RQ, query_part_of(0))
    def block_of(h):
        return pl.ds(pl.multiple_of(h * 2 * DH, 2 * DH), 2 * DH)

    mine = reduced(RO)
    for h in range(2):
        arrived(from_ab.at[RO, h], r_recv.at[RO, 6 + h])
    mine = [(mine[h] + from_ab[RO, h].astype(F32)).astype(BF16) for h in range(2)]
    att_out[:, block_of(head)] = jnp.concatenate(mine, axis=1)

    def piece_at(source, n):
        return pl.ds(pl.multiple_of(source * 2 * DH + n * DH, DH), DH)

    def share(source, base, targets, n):
        for m, target in enumerate(targets):
            remote(att_out.at[:, piece_at(source, n)], att_out.at[:, piece_at(source, n)],
                   h_send.at[2 * (base + m) + n], h_recv.at[2 * source + n], "head", target)

    def wait_share(source, n):
        arrived(att_out.at[:, piece_at(source, n)], h_recv.at[2 * source + n])

    for n in range(2):
        share(head, 0, [head_x] + heads_y, n)
    reduce_b(RK, key_held)
    reduce_b(RQ, query_held)

    def finish(t, out):
        part = reduced(t)
        for h in range(2):
            out[:, h * DH:(h + 1) * DH] = part[h].astype(BF16)

    finish(RV, dv_out)
    for n in range(2):
        wait_share(head_x, n)
        share(head_x, 4, heads_y, n)
    finish(RQ, dq_out)
    finish(RK, dk_out)
    for m in (1, 2, 3):
        for n in range(2):
            wait_share(xh * 4 + (y + m) % 4, n)
            wait_share((1 - xh) * 4 + (y + m) % 4, n)
    for copy in started:
        copy.wait_send()


def body(queries, key_vectors, value_vectors, out_grad, block_order):
    def flat(array):
        return array.reshape(ROWS, 2 * DH)

    vmem = pl.BlockSpec(memory_space=pltpu.VMEM)
    dma = pltpu.SemaphoreType.DMA
    small = jax.ShapeDtypeStruct((ROWS, 2 * DH), BF16)
    outs = pl.pallas_call(
        kernel,
        out_shape=(pltpu.VMEM((ROWS, 16 * DH), BF16),) + (pltpu.VMEM((ROWS, 2 * DH), BF16),) * 3,
        in_specs=[pl.BlockSpec(memory_space=pltpu.SMEM)] + [pl.BlockSpec(memory_space=pl.ANY)] * 4,
        out_specs=(vmem,) * 4,
        scratch_shapes=[
            pltpu.VMEM((4, 4, CHUNK, DH), BF16),
            pltpu.VMEM((4, CHUNK, WIDE), BF16),
            pltpu.VMEM((4, CHUNK, WIDE), F32),
            pltpu.VMEM((1, WIDE), jnp.int32),
            pltpu.VMEM((4, WIDE), F32),
            pltpu.VMEM((4, WIDE), F32),
            pltpu.VMEM((2, WIDE), F32),
            pltpu.VMEM((3, 2, WIDE), F32),
            pltpu.VMEM((1, WIDE), F32),
            pltpu.VMEM((3, 1, WIDE), F32),
            pltpu.VMEM((4, WIDE), F32),
            pltpu.VMEM((DH, WIDE), F32),
            pltpu.VMEM((4, CHUNK, DH), F32),
            pltpu.VMEM((CHUNK, DH), F32),
            pltpu.VMEM((CHUNK, DH), F32),
            pltpu.VMEM((CHUNK, DH), F32),
            pltpu.VMEM((4, 4, CHUNK, DH), BF16),
            pltpu.VMEM((4, CHUNK, DH), BF16),
            pltpu.VMEM((4, 2, ROWS, DH), BF16),
            pltpu.VMEM((4, 2, ROWS, DH), BF16),
            pltpu.VMEM((4, 2, ROWS, DH), BF16),
            pltpu.VMEM((1, 2, ROWS, DH), BF16),
            dma((4, 16)), dma((4, 16)),
            dma((4, 8)), dma((4, 8)),
            dma((3,)), dma((3,)),
            dma((3,)), dma((3,)),
            dma((14,)), dma((16,)),
        ],
        compiler_params=pltpu.CompilerParams(
            collective_id=0, has_side_effects=True, vmem_limit_bytes=56 << 20
        ),
        cost_estimate=pl.CostEstimate(
            flops=12 * WIDE * WIDE * DH, bytes_accessed=3 << 20, transcendentals=WIDE * WIDE
        ),
    )(block_order, flat(queries), flat(key_vectors), flat(value_vectors), flat(out_grad))
    attended, query_grad, key_grad, value_grad = outs
    return (
        attended.reshape(2, SPAN, 16 * DH),
        query_grad.reshape(2, SPAN, 2 * DH),
        key_grad.reshape(2, SPAN, 2 * DH),
        value_grad.reshape(2, SPAN, 2 * DH),
    )


def solution(mesh):
    split = P("blk", None, "head")
    return jax.shard_map(
        body,
        mesh=mesh,
        in_specs=(split, split, split, split, P()),
        out_specs=(P("blk", None, None), split, split, split),
        check_vma=False,
    )
```

time: 76.5 us -> 68 us (0.89)
  the two profiles are of different devices: /device:TPU:5 before, /device:TPU:33 now
where the time goes in v2:
time: 68 us; the launch traced here: 67.9 us
  Pallas kernels  64.4 us (95%)
  local copies, waits for them, and re-layouts  2.94 us (4%)
    pallas_call x1, Pallas kernels, body(): pl.pallas_call(kernel, out_shape=(pltpu.VMEM((ROWS, 16 * DH), BF16),) + (...  64.4 us
    unnamed x4, local copies, waits for them, and re-layouts  2.94 us

profile of v2, /device:TPU:33, one launch (start us, length us, event | category | flops | bytes accessed | tf_op | source)
XLA Modules:
  0.0 67.9 jit_solution(14725916526255636370)
XLA Ops:
  0.6 64.4 %shard_map.84 = (bf16[256,2048]{1,0:T(8,128)(2,1)S(1)}, bf16[256,256]{1,0:T(8,128)(2,1)S(1)}, bf16[256,256]{1,0:T(8,128)(2,1)S(1)}, bf16[256,256]{1,0:T(8,128)(2,1)S(1)}) custom-call(s32[64]{0:T(128)} %order.1, bf16[256,256]{1,0:T(8,128)(2,1)} %bitcast.12, bf16[256,256]{1,0:T(8,128)(2,1)} %bitcast.13, bf16[256,256]{1,0:T(8,128)(2,1)} %bitcast.14, ...), custom_call_target="tpu_custom_call" | custom-call | flops 6442450944 | bytes 3145728 | tf_op jit(solution)/shard_map/pallas_call | solution.py:409
  65.0 1.0 %copy.13 = bf16[2,128,2048]{2,1,0:T(8,128)(2,1)} copy(bf16[2,128,2048]{2,1,0:T(8,128)(2,1)S(1)} %bitcast.8) | data formatting | bytes 2097152
  66.0 0.7 copy.14
  66.6 0.7 copy.15
  67.3 0.7 copy.16

commit v3 on v2

--- a/solution.py
+++ b/solution.py
@@ -105,24 +105,24 @@
         copy.start()
         started.append(copy)
 
-    PIECES = 2
+    PIECES = 1
     PIECE = ROWS // PIECES
 
     def piece_of(r, n):
         return pl.ds(pl.multiple_of(r * ROWS + n * PIECE, PIECE), PIECE)
 
-    def send_to(t, slot, chip, ns):
+    def send_to(t, slot, chip, hs, ns=range(PIECES)):
         for n in ns:
-            for h in range(2):
+            for h in hs:
                 remote(inputs[t].at[pl.ds(n * PIECE, PIECE), lanes(h)], gathered.at[t, slot, piece_of(core, n)],
                        g_send.at[t, (slot * 2 + h) * PIECES + n], g_recv.at[t, (slot * 2 + core) * PIECES + n],
                        "blk", chip + h)
 
-    def send_b(t, ns=range(PIECES)):
-        send_to(t, 2, near_b[t], ns)
-
-    def send_a(t, ns=range(PIECES)):
-        send_to(t, 1, near_a[t], ns)
+    def send_b(t, h):
+        send_to(t, 2, near_b[t], [h])
+
+    def send_a(t, h):
+        send_to(t, 1, near_a[t], [h])
 
     def send_own(t):
         remote(inputs[t].at[:, lanes(other)], gathered.at[t, 0, rows(core)],
@@ -170,12 +170,13 @@
     def dprob_tile(j, i):
         dprobs[j, :, cols(i)] = dot(gathered[TV, j], gathered[TG, i], NT)
 
-    for t in (TK, TQ, TG, TV):
-        send_b(t)
-    for t in (TK, TQ, TG, TV):
-        send_a(t)
+    sequence = ((TK, 0), (TQ, 0), (TK, 1), (TQ, 1), (TG, 0), (TV, 0), (TG, 1), (TV, 1))
+    for t, h in sequence:
+        send_b(t, h)
     for t in (TK, TQ, TG, TV):
         send_own(t)
+    for t, h in sequence:
+        send_a(t, h)
 
     def scores(*tiles):
         for j, i in tiles:
@@ -195,9 +196,7 @@
     wait_slot(TK, 3)
     scores((3, 0), (3, 1), (3, 2))
     wait_slot(TQ, 3)
-    scores((0, 3), (1, 3))
-    wait_forward(TG)
-    scores((2, 3), (3, 3))
+    scores((0, 3), (1, 3), (2, 3), (3, 3))
 
     peers = (q_a, q_b, q_ab)
     tops = [chunk_max[j:j + 1, :] for j in range(4)]
@@ -212,6 +211,7 @@
     def turned_row(ref_row, n):
         return jnp.concatenate([ref_row[:, cols(s ^ (n + 1))] for s in range(4)], axis=1)
 
+    wait_forward(TG)
     wait_forward(TV)
     wait_own(TV)
     wait_own(TG)
@@ -276,23 +276,20 @@
         probs[j, :, cols(i)] = p
         return dot(gathered[TV, j].T, p, NN) if j < 3 else None
 
+    def value_term(j, i):
+        return dot(probs[j, :, cols(i)], gathered[TG, i], NN)
+
     for i in range(4):
         weigh_tile(3, i)
+    for i in range(4):
+        turned[:, cols(i)] = weigh_tile(0, i) + weigh_tile(1, i) + weigh_tile(2, i)
+    for j in (3, 1, 2, 0):
+        key_total[j] = value_term(j, 0) + value_term(j, 1) + value_term(j, 2)
     wait_slot(TG, 3)
-
-    def value_part(j):
-        part = None
-        for i in range(4):
-            term = dot(probs[j, :, cols(i)], gathered[TG, i], NN)
-            part = term if part is None else part + term
-        return part
-
-    part = value_part(3)
+    part = key_total[3] + value_term(3, 3)
     for r in range(2):
         reduce_ab(RV, part[r * ROWS:(r + 1) * ROWS], r)
-    for i in range(4):
-        turned[:, cols(i)] = weigh_tile(0, i) + weigh_tile(1, i) + weigh_tile(2, i)
-    reduce_a(RV, value_part(1))
+    reduce_a(RV, key_total[1] + value_term(1, 3))
     wait_slot(TV, 3)
     for i in range(4):
         o = turned[:, cols(i)] + dot(gathered[TV, 3].T, probs[3, :, cols(i)], NN)
@@ -300,7 +297,6 @@
         delta_out[:, cols(i)] = jnp.sum(o * gathered[TG, i].astype(F32).T, axis=0, keepdims=True)
     for n, peer in enumerate(peers):
         remote(delta_out, delta_in.at[n], d_send.at[n], d_recv.at[n], "blk", peer + core)
-
     for i in (3, 2, 1, 0):
         o = turned[:, cols(i)].T
         if i == 3:
@@ -311,9 +307,8 @@
             reduce_a(RO, o)
         else:
             reduce_own(RO, o)
-    value_held[...] = value_part(2)
-    reduce_own(RV, value_part(0))
-
+    value_held[...] = key_total[2] + value_term(2, 3)
+    reduce_own(RV, key_total[0] + value_term(0, 3))
     for j, i in [(3, 0), (3, 1), (3, 2), (3, 3), (0, 3), (1, 3), (2, 3), (2, 0), (2, 1), (2, 2)]:
         dprob_tile(j, i)
 
@@ -322,6 +317,38 @@
         arrived(delta_in.at[n], d_recv.at[n])
         delta = delta + turned_row(delta_in.at[n], n)
     delta_rows = [delta[:, i * CHUNK:(i + 1) * CHUNK] for i in range(4)]
+
+    def block_of(h):
+        return pl.ds(pl.multiple_of(h * 2 * DH, 2 * DH), 2 * DH)
+
+    def piece_at(source, n):
+        return pl.ds(pl.multiple_of(source * 2 * DH + n * DH, DH), DH)
+
+    near_y = [heads_y[0], heads_y[2]]
+    far_y = heads_y[1]
+    far_xy = (1 - xh) * 4 + (y + 2) % 4
+
+    def share_copies(source, base, targets, n):
+        return [
+            pltpu.make_async_remote_copy(
+                src_ref=att_out.at[:, piece_at(source, n)], dst_ref=att_out.at[:, piece_at(source, n)],
+                send_sem=h_send.at[2 * (base + m) + n], recv_sem=h_recv.at[2 * source + n],
+                device_id={"head": target}, device_id_type=MESH)
+            for m, target in enumerate(targets)
+        ]
+
+    def share(source, base, targets, n):
+        for copy in share_copies(source, base, targets, n):
+            copy.start()
+
+    def share_own():
+        mine = reduced(RO)
+        for h in range(2):
+            arrived(from_ab.at[RO, h], r_recv.at[RO, 6 + h])
+        mine = [(mine[h] + from_ab[RO, h].astype(F32)).astype(BF16) for h in range(2)]
+        att_out[:, block_of(head)] = jnp.concatenate(mine, axis=1)
+        for n in range(2):
+            share(head, 0, [head_x, far_y] + near_y, n)
 
     fresh_q = set()
 
@@ -348,6 +375,11 @@
         reduce_ab(RQ, part[r * ROWS:(r + 1) * ROWS], r)
     key_held[...] = (key_total[2] + sum(grad_tile(2, i) for i in range(3))) * SCALE
     reduce_b(RV, value_held)
+
+    @pl.when(core == 1)
+    def _():
+        share_own()
+
     for j in range(2):
         key_total[j] += grad_tile(j, 2)
     query_held[...] = query_part_of(2)
@@ -355,30 +387,16 @@
     reduce_own(RK, (key_total[0] + sum(grad_tile(0, i) for i in range(2))) * SCALE)
     reduce_a(RQ, query_part_of(1))
     reduce_own(RQ, query_part_of(0))
-    def block_of(h):
-        return pl.ds(pl.multiple_of(h * 2 * DH, 2 * DH), 2 * DH)
-
-    mine = reduced(RO)
-    for h in range(2):
-        arrived(from_ab.at[RO, h], r_recv.at[RO, 6 + h])
-    mine = [(mine[h] + from_ab[RO, h].astype(F32)).astype(BF16) for h in range(2)]
-    att_out[:, block_of(head)] = jnp.concatenate(mine, axis=1)
-
-    def piece_at(source, n):
-        return pl.ds(pl.multiple_of(source * 2 * DH + n * DH, DH), DH)
-
-    def share(source, base, targets, n):
-        for m, target in enumerate(targets):
-            remote(att_out.at[:, piece_at(source, n)], att_out.at[:, piece_at(source, n)],
-                   h_send.at[2 * (base + m) + n], h_recv.at[2 * source + n], "head", target)
+    reduce_b(RK, key_held)
+    reduce_b(RQ, query_held)
+
+    @pl.when(core == 0)
+    def _():
+        share_own()
+
 
     def wait_share(source, n):
         arrived(att_out.at[:, piece_at(source, n)], h_recv.at[2 * source + n])
-
-    for n in range(2):
-        share(head, 0, [head_x] + heads_y, n)
-    reduce_b(RK, key_held)
-    reduce_b(RQ, query_held)
 
     def finish(t, out):
         part = reduced(t)
@@ -388,13 +406,20 @@
     finish(RV, dv_out)
     for n in range(2):
         wait_share(head_x, n)
-        share(head_x, 4, heads_y, n)
+        share(head_x, 4, near_y, n)
+        wait_share(far_y, n)
+        share(far_y, 6, [head_x], n)
     finish(RQ, dq_out)
     finish(RK, dk_out)
-    for m in (1, 2, 3):
-        for n in range(2):
+    for n in range(2):
+        wait_share(far_xy, n)
+        for m in (1, 3):
             wait_share(xh * 4 + (y + m) % 4, n)
             wait_share((1 - xh) * 4 + (y + m) % 4, n)
+    for n in range(2):
+        started.extend(share_copies(head, 0, [head_x, far_y] + near_y, n))
+        started.extend(share_copies(head_x, 4, near_y, n))
+        started.extend(share_copies(far_y, 6, [head_x], n))
     for copy in started:
         copy.wait_send()
 

time: 68 us -> 63.6 us (0.935)
  Pallas kernels: 64.4 us -> 60 us
    pallas_call x1, Pallas kernels: 64.4 us -> 60 us  [body(): pl.pallas_call(kernel, out_shape=(pltpu.VMEM((ROWS, 16 * DH), BF16),) + (...]
where the time goes in v3:
time: 63.6 us
  Pallas kernels  60 us (94%)
  local copies, waits for them, and re-layouts  2.94 us (5%)
  between operations  0.64 us (1%)
    pallas_call x1, Pallas kernels, body(): pl.pallas_call(kernel, out_shape=(pltpu.VMEM((ROWS, 16 * DH), BF16),) + (...  60 us
    unnamed x4, local copies, waits for them, and re-layouts  2.94 us

profile of v3, /device:TPU:33, one launch (start us, length us, event | category | flops | bytes accessed | tf_op | source)
XLA Modules:
  0.0 63.6 jit_solution(5484191445738319736)
XLA Ops:
  0.6 60.0 %shard_map.84 = (bf16[256,2048]{1,0:T(8,128)(2,1)S(1)}, bf16[256,256]{1,0:T(8,128)(2,1)S(1)}, bf16[256,256]{1,0:T(8,128)(2,1)S(1)}, bf16[256,256]{1,0:T(8,128)(2,1)S(1)}) custom-call(s32[64]{0:T(128)} %order.1, bf16[256,256]{1,0:T(8,128)(2,1)} %bitcast.12, bf16[256,256]{1,0:T(8,128)(2,1)} %bitcast.13, bf16[256,256]{1,0:T(8,128)(2,1)} %bitcast.14, ...), custom_call_target="tpu_custom_call" | custom-call | flops 6442450944 | bytes 3145728 | tf_op jit(solution)/shard_map/pallas_call | solution.py:434
  60.6 1.0 %copy.13 = bf16[2,128,2048]{2,1,0:T(8,128)(2,1)} copy(bf16[2,128,2048]{2,1,0:T(8,128)(2,1)S(1)} %bitcast.8) | data formatting | bytes 2097152
  61.6 0.7 %copy.14 = bf16[2,128,256]{2,1,0:T(8,128)(2,1)} copy(bf16[2,128,256]{2,1,0:T(8,128)(2,1)S(1)} %bitcast.11) | data formatting | bytes 262144
  62.2 0.7 %copy.15 = bf16[2,128,256]{2,1,0:T(8,128)(2,1)} copy(bf16[2,128,256]{2,1,0:T(8,128)(2,1)S(1)} %bitcast.10) | data formatting | bytes 262144
  62.9 0.7 %copy.16 = bf16[2,128,256]{2,1,0:T(8,128)(2,1)} copy(bf16[2,128,256]{2,1,0:T(8,128)(2,1)S(1)} %bitcast.9) | data formatting | bytes 262144

commit v4 on v3

--- a/solution.py
+++ b/solution.py
@@ -365,14 +365,26 @@
     def query_part_of(i):
         return turned[:, cols(i)].T * SCALE
 
+    def first_key_tile(i, part):
+        ds = (probs[3, part, cols(i)].astype(F32) * (dprobs[3, part, cols(i)] - delta_rows[i])).astype(BF16)
+        probs[3, part, cols(i)] = ds
+        return dot(ds, gathered[TQ, i], NN)
+
+    def first_query_tile(i):
+        turned[:, cols(i)] = dot(gathered[TK, 3].T, probs[3, :, cols(i)], NN)
+        fresh_q.add(i)
+
     for r in range(2):
-        part = sum(grad_tile(3, i, halves[r]) for i in range(4))
+        part = sum(first_key_tile(i, halves[r]) for i in range(4))
         reduce_ab(RK, part * SCALE, r)
+    first_query_tile(3)
     for j in range(3):
         key_total[j] = grad_tile(j, 3)
     part = query_part_of(3)
     for r in range(2):
         reduce_ab(RQ, part[r * ROWS:(r + 1) * ROWS], r)
+    for i in range(3):
+        first_query_tile(i)
     key_held[...] = (key_total[2] + sum(grad_tile(2, i) for i in range(3))) * SCALE
     reduce_b(RV, value_held)
 

time: 63.6 us -> 63.5 us (level)
  no operation moved by 1% of the time
where the time goes in v4:
time: 63.5 us; the launch traced here: 63.4 us
  Pallas kernels  59.8 us (94%)
  local copies, waits for them, and re-layouts  2.94 us (5%)
  between operations  0.64 us (1%)
    pallas_call x1, Pallas kernels, body(): pl.pallas_call(kernel, out_shape=(pltpu.VMEM((ROWS, 16 * DH), BF16),) + (...  59.8 us
    unnamed x4, local copies, waits for them, and re-layouts  2.94 us

profile of v4, /device:TPU:33, one launch (start us, length us, event | category | flops | bytes accessed | tf_op | source)
XLA Modules:
  0.0 63.4 jit_solution(3053471824393940283)
XLA Ops:
  0.6 59.8 %shard_map.84 = (bf16[256,2048]{1,0:T(8,128)(2,1)S(1)}, bf16[256,256]{1,0:T(8,128)(2,1)S(1)}, bf16[256,256]{1,0:T(8,128)(2,1)S(1)}, bf16[256,256]{1,0:T(8,128)(2,1)S(1)}) custom-call(s32[64]{0:T(128)} %order.1, bf16[256,256]{1,0:T(8,128)(2,1)} %bitcast.12, bf16[256,256]{1,0:T(8,128)(2,1)} %bitcast.13, bf16[256,256]{1,0:T(8,128)(2,1)} %bitcast.14, ...), custom_call_target="tpu_custom_call" | custom-call | flops 6442450944 | bytes 3145728 | tf_op jit(solution)/shard_map/pallas_call | solution.py:446
  60.4 1.0 %copy.13 = bf16[2,128,2048]{2,1,0:T(8,128)(2,1)} copy(bf16[2,128,2048]{2,1,0:T(8,128)(2,1)S(1)} %bitcast.8) | data formatting | bytes 2097152
  61.4 0.7 %copy.14 = bf16[2,128,256]{2,1,0:T(8,128)(2,1)} copy(bf16[2,128,256]{2,1,0:T(8,128)(2,1)S(1)} %bitcast.11) | data formatting | bytes 262144
  62.1 0.7 %copy.15 = bf16[2,128,256]{2,1,0:T(8,128)(2,1)} copy(bf16[2,128,256]{2,1,0:T(8,128)(2,1)S(1)} %bitcast.10) | data formatting | bytes 262144
  62.7 0.7 %copy.16 = bf16[2,128,256]{2,1,0:T(8,128)(2,1)} copy(bf16[2,128,256]{2,1,0:T(8,128)(2,1)S(1)} %bitcast.9) | data formatting | bytes 262144
